TPU v7x, 256 devices: a whole 4x4x8 slice. The times are simulated.
256 devices in a mesh: qrow: 8 (over x_hi, y), kcol: 32 (over z, x_lo, core).
Axes of the slice: x: 4 (x_hi: 2, x_lo: 2; x = x_hi * 2 + x_lo), y: 4, z: 8, core: 2. Of those that a mesh axis runs over, the one named last changes fastest.
Arguments:
- homolog_source_features: bfloat16 [16, 768, 256], P(None, ('qrow', 'kcol')), may hold values from -6 to 6
- homolog_target_features: bfloat16 [16, 2048, 256], P('qrow', 'kcol'), may hold values from -6 to 6
- first_factor_matrix: bfloat16 [256, 32], replicated, may hold values from -0.375 to 0.375
- second_factor_matrix: bfloat16 [256, 32], replicated, may hold values from -0.375 to 0.375
- output_weight: bfloat16 [1024, 128], replicated, may hold values from -0.1875 to 0.1875
- output_bias: float32 [128], replicated, may hold values from -4 to 4
- pair_cotangent: bfloat16 [768, 2048, 128], P('qrow', 'kcol'), may hold values from -6 to 6
Outputs:
- pair_update: bfloat16 [768, 2048, 128], P('qrow', 'kcol')
- grad_rows: bfloat16 [16, 768, 256], P(None, ('qrow', 'kcol'))
- grad_cols: bfloat16 [16, 2048, 256], P('qrow', 'kcol')
- grad_w_out: float32 [1024, 128], replicated
- grad_b_out: float32 [128], replicated
- grad_w_left: float32 [256, 32], replicated
- grad_w_right: float32 [256, 32], replicated
All inputs are finite; a program needn't handle non-finite values.
Results may differ from a plain program's by a relative error of at most 0.033.
Values may be sent and summed in bfloat16 or wider, within the bound.
A program may use at most 128 MiB of HBM per device.

v0:
```python
import jax
import jax.numpy as jnp
from jax import lax
from jax.sharding import PartitionSpec as P


def layer_normalize(x):
    values = x.astype(jnp.float32)
    center = values - jnp.mean(values, axis=-1, keepdims=True)
    inverse = lax.rsqrt(jnp.mean(center * center, axis=-1, keepdims=True) + 1e-05)
    return (center * inverse, inverse)


def norm_back(grad_norm, normed, inverse):
    first = jnp.mean(grad_norm, axis=-1, keepdims=True)
    second = jnp.mean(grad_norm * normed, axis=-1, keepdims=True)
    return (inverse * (grad_norm - first - normed * second)).astype(jnp.bfloat16)


def local(
    homolog_source_features,
    homolog_target_features,
    first_factor_matrix,
    second_factor_matrix,
    output_weight,
    output_bias,
    pair_cotangent,
):
    sequence_count = homolog_source_features.shape[0]
    averaging_factor = 1.0 / sequence_count
    centered_query_rows, inverse_std_rows = layer_normalize(homolog_source_features)
    centered_key_columns, inverse_std_columns = layer_normalize(homolog_target_features)
    ln_rows = centered_query_rows.astype(jnp.bfloat16)
    ln_cols = centered_key_columns.astype(jnp.bfloat16)
    left_local = jnp.dot(ln_rows, first_factor_matrix, preferred_element_type=jnp.float32).astype(
        jnp.bfloat16
    )
    right_local = jnp.dot(ln_cols, second_factor_matrix, preferred_element_type=jnp.float32).astype(
        jnp.bfloat16
    )
    left = lax.all_gather(left_local, "kcol", axis=1, tiled=True)
    right = lax.all_gather(right_local, "qrow", axis=0, tiled=True)
    query_rows = left.shape[1]
    key_cols = right.shape[1]
    chans = left.shape[2]
    outer = (
        jnp.einsum("sic,sje->ijce", left, right, preferred_element_type=jnp.float32)
        * averaging_factor
    )
    outer = outer.astype(jnp.bfloat16).reshape(query_rows * key_cols, chans * chans)
    pair = jnp.dot(outer, output_weight, preferred_element_type=jnp.float32) + output_bias
    pair_update = pair.astype(jnp.bfloat16).reshape(query_rows, key_cols, -1)
    grad_flat = pair_cotangent.reshape(query_rows * key_cols, -1)
    d_outer = jnp.dot(grad_flat, output_weight.T, preferred_element_type=jnp.float32).astype(
        jnp.bfloat16
    )
    d_outer = d_outer.reshape(query_rows, key_cols, chans, chans)
    left_sums = lax.psum_scatter(
        (
            jnp.einsum("ijce,sje->isc", d_outer, right, preferred_element_type=jnp.float32)
            * averaging_factor
        ).astype(jnp.bfloat16),
        "kcol",
        scatter_dimension=0,
        tiled=True,
    ).astype(jnp.float32)
    first_factor_gradient = jnp.transpose(left_sums, (1, 0, 2)).astype(jnp.bfloat16)
    d_right = lax.psum_scatter(
        (
            jnp.einsum("ijce,sic->sje", d_outer, left, preferred_element_type=jnp.float32)
            * averaging_factor
        ).astype(jnp.bfloat16),
        "qrow",
        scatter_dimension=0,
        tiled=True,
    )
    term_out = jnp.einsum("nk,np->kp", outer, grad_flat, preferred_element_type=jnp.float32)
    term_bias = jnp.sum(grad_flat.astype(jnp.float32), axis=0)
    term_left = jnp.einsum(
        "sim,sic->mc", ln_rows, first_factor_gradient, preferred_element_type=jnp.float32
    )
    term_right = jnp.einsum("sim,sic->mc", ln_cols, d_right, preferred_element_type=jnp.float32)
    grad_w_out, grad_b_out, grad_w_left, grad_w_right = lax.psum(
        (term_out, term_bias, term_left, term_right), ("qrow", "kcol")
    )
    back_rows = jnp.dot(
        first_factor_gradient, first_factor_matrix.T, preferred_element_type=jnp.float32
    )
    back_cols = jnp.dot(d_right, second_factor_matrix.T, preferred_element_type=jnp.float32)
    grad_rows = norm_back(back_rows, centered_query_rows, inverse_std_rows)
    grad_cols = norm_back(back_cols, centered_key_columns, inverse_std_columns)
    return (pair_update, grad_rows, grad_cols, grad_w_out, grad_b_out, grad_w_left, grad_w_right)


def solution(mesh):
    return jax.shard_map(
        local,
        mesh=mesh,
        in_specs=(
            P(None, ("qrow", "kcol"), None),
            P("qrow", "kcol", None),
            P(),
            P(),
            P(),
            P(),
            P("qrow", "kcol", None),
        ),
        out_specs=(
            P("qrow", "kcol", None),
            P(None, ("qrow", "kcol"), None),
            P("qrow", "kcol", None),
            P(),
            P(),
            P(),
            P(),
        ),
        check_vma=False,
    )
```

profile of v0, /device:TPU:1, one launch (start us, length us, event | category | flops | bytes accessed | tf_op | source)
XLA Modules:
  0.0 821.7 jit_solution(13778913030276583024)
XLA Ops:
  7.2 0.9 convert_reduce_fusion.2
  8.1 0.9 fusion.31
  9.0 0.9 convolution_convert_fusion.2
  9.9 39.5 %all_gather.7 = bf16[16,96,32]{2,0,1:T(8,128)(2,1)S(1)} all-gather(bf16[16,3,32]{2,0,1:T(8,128)(2,1)S(1)} %convolution_convert_fusion.2), channel_id=1, replica_groups=mesh['qrow'=8,'kcol'=32] {'kcol'}, dimensions={1}, use_global_device_ids=true | all-gather | bytes 101376 | tf_op jit(solution)/shard_map/all_gather | solution.py:41
  49.5 1.3 copy.37
  50.7 7.9 convolution_convert_fusion
  58.7 16.7 %copy.39 = bf16[6144,1024]{0,1:T(8,128)(2,1)} copy(bf16[6144,1024]{1,0:T(8,128)(2,1)} %convolution_convert_fusion) | data formatting | bytes 25165824 | tf_op jit(solution)/shard_map/convert_element_type | solution.py:54
  75.4 34.2 %reshape.70 = bf16[96,64,32,32]{1,0,3,2:T(8,128)(2,1)} reshape(bf16[6144,1024]{0,1:T(8,128)(2,1)} %copy.39) | data formatting | bytes 25165824 | tf_op jit(solution)/shard_map/reshape | solution.py:57
  109.6 10.0 %fusion.5 = bf16[16,64,32]{1,0,2:T(8,128)(2,1)S(1)} fusion(bf16[96,64,32,32]{1,0,3,2:T(8,128)(2,1)} %reshape.70, bf16[16,96,32]{0,1,2:T(8,128)(2,1)S(1)} %copy.37), kind=kOutput, calls=%fused_computation.11 | convolution fusion | flops 201392128 | bytes 12746752 | tf_op jit(solution)/shard_map/ijce,sic->sje/dot_general | solution.py:70
  119.6 0.7 copy.45
  120.9 28.4 %all_gather.6 = bf16[16,64,32]{1,2,0:T(8,128)(2,1)S(1)} all-gather(bf16[2,64,32]{1,2,0:T(8,128)(2,1)S(1)} %convolution_convert_fusion.1), channel_id=1, replica_groups=mesh['qrow'=8,'kcol'=32] {'qrow'}, dimensions={0}, use_global_device_ids=true | all-gather | bytes 73728 | tf_op jit(solution)/shard_map/all_gather | solution.py:42
  149.4 12.4 %fusion.6 = bf16[96,16,32]{0,1,2:T(8,128)(2,1)S(1)} fusion(bf16[96,64,32,32]{1,0,3,2:T(8,128)(2,1)} %reshape.70, bf16[16,64,32]{1,2,0:T(8,128)(2,1)S(1)} %all_gather.6), kind=kOutput, calls=%fused_computation.12 | convolution fusion | flops 201424896 | bytes 12746752 | tf_op jit(solution)/shard_map/ijce,sje->isc/dot_general | solution.py:60
  161.8 1.1 copy.42
  162.9 0.2 all-reduce.6.cloned.1.call-start
  163.2 8.1 fusion
  171.3 1.3 convert_reduce_fusion
  172.6 27.8 %copy.38 = bf16[96,64,32,32]{1,0,3,2:T(8,128)(2,1)} copy(bf16[96,64,32,32]{0,1,2,3:T(8,128)(2,1)} %fusion) | data formatting | bytes 25165824 | tf_op jit(solution)/shard_map/convert_element_type | solution.py:50
  200.5 32.7 %reshape.67 = bf16[6144,1024]{0,1:T(8,128)(2,1)} reshape(bf16[96,64,32,32]{1,0,3,2:T(8,128)(2,1)} %copy.38) | data formatting | bytes 25165824 | tf_op jit(solution)/shard_map/reshape | solution.py:50
  233.2 1.6 convolution_bitcast_fusion.2
  234.8 71.1 %reduce-scatter.3.cloned.1.call-done = bf16[3,16,32]{2,1,0:T(8,128)(2,1)} async-done(((bf16[96,16,32]{2,1,0:T(8,128)(2,1)}), bf16[3,16,32]{2,1,0:T(8,128)(2,1)}) %reduce-scatter.3.cloned.1.call-update) | async-done | bytes 3088 | tf_op jit(solution)/shard_map/reduce_scatter | solution.py:58
  305.9 1.5 convolution_bitcast_fusion.3
  307.5 7.2 fusion.46
  314.8 9.2 %fusion.1 = bf16[6144,128]{1,0:T(8,128)(2,1)} fusion(bf16[6144,1024]{0,1:T(8,128)(2,1)} %reshape.67, bf16[1024,128]{1,0:T(8,128)(2,1)S(1)} %copy-done, f32[128]{0:T(128)S(1)} %copy-done.8), kind=kOutput, calls=%fused_computation.4 | convolution fusion | flops 1612185600 | bytes 14418432 | tf_op jit(solution)/shard_map/dot_general | solution.py:51
  324.0 0.3 fusion.44
  324.3 0.8 fusion.17
  325.3 0.7 fusion.30
  326.0 229.7 %all-reduce.6.cloned.1.call-done = (f32[128]{0:T(128)}, f32[256,32]{0,1:T(8,128)}, f32[256,32]{0,1:T(8,128)}) async-done(((f32[128]{0:T(128)}, f32[256,32]{0,1:T(8,128)}, f32[256,32]{0,1:T(8,128)}), (f32[128]{0:T(128)}, f32[256,32]{0,1:T(8,128)}, f32[256,32]{0,1:T(8,128)})) %all-reduce.6.cloned.1.call-update) | async-done | bytes 66064 | tf_op jit(solution)/shard_map/psum | solution.py:83
  555.7 253.8 %all-reduce.4.cloned.1.call-done = f32[1024,128]{1,0:T(8,128)} async-done(((f32[1024,128]{1,0:T(8,128)}), f32[1024,128]{1,0:T(8,128)}) %all-reduce.4.cloned.1.call-update) | async-done | bytes 524304 | tf_op jit(solution)/shard_map/psum | solution.py:83
  809.5 1.9 copy.64
  811.3 1.1 copy.65
  812.5 1.4 copy.66
  813.8 1.4 copy.67
  (36 shorter events, 1.0 us)
Async XLA Ops:
  7.2 43.6 %copy-start = (bf16[1024,128]{1,0:T(8,128)(2,1)S(1)}, bf16[1024,128]{1,0:T(8,128)(2,1)}, u32[]{:S(2)}) copy-start(bf16[1024,128]{1,0:T(8,128)(2,1)} %param.11) | copy-start | bytes 786436
  7.2 226.0 %reduce-scatter.5.cloned.1.call-start = ((), (), s32[]{:S(2)}) async-start(), calls=%async_computation.3 | async-start | bytes 147456 | tf_op jit(solution)/shard_map/reduce_scatter | solution.py:68
  109.6 10.8 %copy-start.2 = (bf16[2,64,256]{2,1,0:T(8,128)(2,1)S(1)}, bf16[2,64,256]{2,1,0:T(8,128)(2,1)}, u32[]{:S(2)}) copy-start(bf16[2,64,256]{2,1,0:T(8,128)(2,1)} %param.8) | copy-start | bytes 196612
  109.6 11.1 %copy-start.4 = (bf16[256,32]{0,1:T(8,128)(2,1)S(1)}, bf16[256,32]{0,1:T(8,128)(2,1)}, u32[]{:S(2)}) copy-start(bf16[256,32]{0,1:T(8,128)(2,1)} %param.10) | copy-start | bytes 49156
  120.3 185.6 %reduce-scatter.3.cloned.1.call-start = ((), (), s32[]{:S(2)}) async-start(), calls=%async_computation.2 | async-start | bytes 405504 | tf_op jit(solution)/shard_map/reduce_scatter | solution.py:58
  161.8 9.5 %copy-start.1 = (bf16[96,64,128]{2,1,0:T(8,128)(2,1)S(1)}, bf16[96,64,128]{2,1,0:T(8,128)(2,1)}, u32[]{:S(2)}) copy-start(bf16[96,64,128]{2,1,0:T(8,128)(2,1)} %param.13) | copy-start | bytes 4718596
  162.9 392.7 %all-reduce.6.cloned.1.call-start = ((), (), s32[]{:S(2)}) async-start(), calls=%async_computation.5 | async-start | bytes 132096 | tf_op jit(solution)/shard_map/psum | solution.py:83
  200.5 105.4 %copy-start.3 = (bf16[16,3,256]{2,0,1:T(8,128)(2,1)S(1)}, bf16[16,3,256]{2,0,1:T(8,128)(2,1)}, u32[]{:S(2)}) copy-start(bf16[16,3,256]{2,0,1:T(8,128)(2,1)} %param.7) | copy-start | bytes 73732
  233.2 81.5 %copy-start.8 = (f32[128]{0:T(128)S(1)}, f32[128]{0:T(128)}, u32[]{:S(2)}) copy-start(f32[128]{0:T(128)} %param.12) | copy-start | bytes 1540
  307.5 502.0 %all-reduce.4.cloned.1.call-start = ((), (), s32[]{:S(2)}) async-start(), calls=%async_computation.4 | async-start | bytes 1048576 | tf_op jit(solution)/shard_map/psum | solution.py:83
  314.7 9.2 %copy-start.5 = (bf16[2,64,32]{1,2,0:T(8,128)(2,1)S(1)}, bf16[2,64,32]{1,2,0:T(8,128)(2,1)}, u32[]{:S(2)}) copy-start(bf16[2,64,32]{1,2,0:T(8,128)(2,1)} %reduce-scatter.5.cloned.1.call-done) | copy-start | bytes 24580
  314.7 10.3 %copy-start.6 = (bf16[256,32]{0,1:T(8,128)(2,1)S(1)}, bf16[256,32]{0,1:T(8,128)(2,1)}, u32[]{:S(2)}) copy-start(bf16[256,32]{0,1:T(8,128)(2,1)} %param.9) | copy-start | bytes 49156
  314.7 10.3 %copy-start.7 = (bf16[3,16,32]{2,1,0:T(8,128)(2,1)S(1)}, bf16[3,16,32]{2,1,0:T(8,128)(2,1)}, u32[]{:S(2)}) copy-start(bf16[3,16,32]{2,1,0:T(8,128)(2,1)} %reduce-scatter.3.cloned.1.call-done) | copy-start | bytes 9220
Sparse Core Ops, SparseCore 0:
  120.5 69.5 reduce-scatter.4
  193.1 112.7 reduce-scatter.2
  313.5 242.1 all-reduce.5
  562.4 246.9 all-reduce.3
where the time goes:
time: 826 us; the launch traced here: 822 us
  waiting for transfers between devices  555 us (67%)
  local copies, waits for them, and re-layouts  120 us (15%)
  blocking collectives  68 us (8%)
  matrix products  59.7 us (7%)
  between operations  13.9 us (2%)
    psum x2, waiting for transfers between devices, local(): lax.psum((term_out, term_bias, term_left, term_right), ('qrow', 'kcol'))  483 us
    reduce_scatter x1, waiting for transfers between devices, local(): lax.psum_scatter((jnp.einsum('ijce,sje->isc', d_outer, right, preferred_e...  71.1 us
    all_gather x1, blocking collectives, local(): left = lax.all_gather(left_local, 'kcol', axis=1, tiled=True)  39.5 us
    reshape x1, local copies, waits for them, and re-layouts, local(): d_outer = d_outer.reshape(query_rows, key_cols, chans, chans)  34.2 us
    reshape x1, local copies, waits for them, and re-layouts, local(): outer.astype(jnp.bfloat16).reshape(query_rows * key_cols, chans * chans)  32.7 us
    all_gather x1, blocking collectives, local(): right = lax.all_gather(right_local, 'qrow', axis=0, tiled=True)  28.4 us
    convert_element_type x1, local copies, waits for them, and re-layouts, local(): outer.astype(jnp.bfloat16).reshape(query_rows * key_cols, chans * chans)  27.8 us
    convert_element_type x1, local copies, waits for them, and re-layouts, local(): jnp.dot(grad_flat, output_weight.T, preferred_element_type=jnp.float32)  16.7 us
  transfers between devices with their start and end apart: 4, of which 3 were waited for; matrix products, arithmetic and copies ran while one was open for 13% of the time, Pallas kernels for 0%

commit v1 on v0

v1 whole, which is shorter than its diff:
```python
import jax
import jax.numpy as jnp
from jax import lax
from jax.experimental import pallas as pl
from jax.experimental.pallas import tpu as pltpu
from jax.sharding import PartitionSpec as P

F32, BF16 = jnp.float32, jnp.bfloat16
MESH = pl.DeviceIdType.MESH
EPS = 1e-05

NQ, NK, NZ, NXY = 8, 32, 8, 16


def nn(a, b):
    return jnp.dot(a, b, preferred_element_type=F32)


def nt(a, b):
    return lax.dot_general(a, b, (((1,), (1,)), ((), ())), preferred_element_type=F32)


def mean_of(v):
    return jnp.mean(v, axis=-1, keepdims=True)


def normalize(v):
    center = v - mean_of(v)
    inv = lax.rsqrt(mean_of(center * center) + EPS)
    return center * inv, inv


def norm_back(g, hat, inv):
    return inv * (g - mean_of(g) - hat * mean_of(g * hat))


def iota(shape, dim):
    return lax.broadcasted_iota(jnp.int32, shape, dim)


def loop(lo, hi, body):
    def step(d, carry):
        body(d)
        return carry

    lax.fori_loop(lo, hi, step, 0)


def kernel(
    xs_ref, xc_ref, w1_ref, w2_ref, w_ref, b_ref, g_hbm,
    pair_hbm, grows_ref, gcols_ref, gw_ref, gb_ref, gwl_ref, gwr_ref,
    g, gs, pf, po, w4, w2t, xsf, hat_r, hat_c, inv_r, inv_c,
    rf, rm, rl, ap, bp, lf, lmf, lm, lt, dlf, dsf, drf, gwp,
    rbuf, lbuf, sdl, rdl, sdr, rdr,
    bsend, bcore, bxy, bz,
    sgc, rgc, sgx, rgx, rgz, fgw,
    sm, ssm, rsc, rsx, rsz, fsm,
    lsem, ssem, rsem,
):
    me_q, me_k = lax.axis_index("qrow"), lax.axis_index("kcol")
    me_z = lax.div(me_k, 4)
    me_x = lax.rem(lax.div(me_k, 2), 2)
    core = lax.rem(me_k, 2)
    me_p = me_x * 8 + me_q

    def at_k(d):
        k = lax.rem(me_k + d, NK)
        return k, (me_q, k)

    def at_q(d):
        q = lax.rem(me_q + d, NQ)
        return q, (q, me_k)

    def at_p(d):
        p = lax.rem(me_p + d, NXY)
        return p, (lax.rem(p, 8), me_z * 4 + lax.div(p, 8) * 2 + core)

    def at_z(d):
        z = lax.rem(me_z + d, NZ)
        return z, (me_q, z * 4 + me_x * 2 + core)

    mate = (me_q, me_k + 1 - 2 * core)

    def send(src, dst, n, device):
        pltpu.make_async_remote_copy(
            src_ref=src, dst_ref=dst, send_sem=ssem.at[n], recv_sem=rsem.at[n],
            device_id=device, device_id_type=MESH,
        ).start()

    def arrived(ref, n):
        pltpu.make_async_copy(ref, ref, rsem.at[n]).wait()

    def sent(ref, n):
        pltpu.make_async_copy(ref, ref, ssem.at[n]).wait()

    load_g = pltpu.make_async_copy(g_hbm, g, lsem.at[0])
    load_g.start()

    barrier = pltpu.get_barrier_semaphore()

    def greet(device):
        pl.semaphore_signal(barrier, inc=1, device_id=device, device_id_type=MESH)

    loop(1, NK, lambda d: greet(at_k(d)[1]))
    loop(1, NQ, lambda d: greet(at_q(d)[1]))
    loop(1, NQ, lambda d: greet((at_q(d)[0], me_z * 4 + (1 - me_x) * 2 + core)))

    lane_group = lax.shift_right_logical(iota((16, 128), 1), 5)
    lane_s = jnp.bitwise_and(iota((16, 512), 1), 15) == iota((16, 512), 0)
    fold = (lax.shift_right_logical(iota((128, 512), 1), 4) == iota((128, 512), 0)).astype(BF16)

    spread = (jnp.bitwise_and(iota((32, 128), 1), 31) == iota((32, 128), 0)).astype(BF16)
    w2t[...] = nn(w2_ref[...], spread).astype(BF16)
    hat, inv = normalize(xc_ref[...].astype(F32).reshape(128, 256))
    hat_c[...] = hat
    inv_c[...] = jnp.broadcast_to(inv, (128, 128))
    right = nn(hat.astype(BF16), w2t[...]).astype(BF16).astype(F32)
    tiles = []
    for t in range(2):
        tile = right[t * 64 : t * 64 + 16, :]
        for jg in range(1, 4):
            tile = jnp.where(lane_group == jg, right[t * 64 + jg * 16 : t * 64 + jg * 16 + 16, :], tile)
        tiles.append(tile)
    rbuf[me_q] = jnp.concatenate(tiles, axis=0).astype(BF16)

    for h in range(2):
        for s in range(16):
            xsf[h, s * 8 : s * 8 + 3, :] = xs_ref[s, :, h * 128 : (h + 1) * 128].astype(F32)
    rows = jnp.concatenate(
        [
            jnp.concatenate([xsf[h, pl.ds(i3, 16, stride=8), :] for h in range(2)], axis=1)
            for i3 in range(3)
        ],
        axis=0,
    )
    hat, inv = normalize(rows)
    hat_r[...] = hat
    inv_r[...] = jnp.broadcast_to(inv, (48, 128))
    left = nn(hat.astype(BF16), w1_ref[...]).astype(BF16)
    tile = jnp.zeros((16, 128), F32)
    for i3 in range(3):
        wide = nn(left[i3 * 16 : i3 * 16 + 16, :], fold[0:32, :])
        row = jnp.sum(jnp.where(lane_s, wide, 0.0), axis=0, keepdims=True)
        for cq in range(4):
            piece = jnp.broadcast_to(row[:, cq * 128 : (cq + 1) * 128], (16, 128))
            tile = jnp.where(iota((16, 128), 0) == i3 * 4 + cq, piece, tile)
    lbuf[me_k] = tile.astype(BF16)

    for c in range(32):
        block = w_ref[c * 32 : (c + 1) * 32, :]
        for jg in range(4):
            w4[jg * 32 : (jg + 1) * 32, c * 128 : (c + 1) * 128] = block

    load_g.wait()

    def widen(n, total):
        for u in range(4):
            v = g[4 * n + u].astype(F32)
            pf[pl.ds(pl.multiple_of((4 * n + u) * 64, 64), 64), :] = v
            total = total + v
        return total

    total = lax.fori_loop(0, 24, widen, jnp.zeros((64, 128), F32))
    bsend[...] = jnp.broadcast_to(jnp.sum(total, axis=0, keepdims=True), (8, 128))

    def turn(n):
        for u in range(4):
            lanes = pl.ds(pl.multiple_of((4 * n + u) * 128, 128), 128)
            gs[:, lanes] = pf[pl.ds(4 * n + u, 96, stride=64), :].astype(BF16)

    loop(0, 16, turn)

    pl.semaphore_wait(barrier, NK + 2 * NQ - 3)

    loop(1, NQ, lambda d: send(rbuf.at[me_q], rbuf.at[me_q], 0, at_q(d)[1]))
    loop(1, NK, lambda d: send(lbuf.at[me_k], lbuf.at[me_k], 1, at_k(d)[1]))
    send(bsend, bcore, 2, mate)

    arrived(rbuf.at[pl.ds(0, NQ - 1)], 0)
    for s in range(16):
        part = rbuf[s // 2, (s % 2) * 16 : (s % 2) * 16 + 16, :].astype(F32)
        rf[pl.ds(s, 16, stride=16), :] = part * (1.0 / 16.0)
    rx = rf[...]
    group = lax.shift_right_logical(iota((256, 128), 1), 5)
    for jg in range(4):
        rm[jg * 256 : (jg + 1) * 256, :] = jnp.where(group == jg, rx, 0.0).astype(BF16)
    rxt = rx.T
    for jg in range(4):
        rl[:, jg * 256 : (jg + 1) * 256] = rxt[jg * 32 : (jg + 1) * 32, :].astype(BF16)

    def make_a(jg):
        for cc in range(16):
            r = nn(
                rm[pl.ds(pl.multiple_of(jg * 256, 256), 256), :],
                w4[:, cc * 256 : (cc + 1) * 256],
            ).astype(BF16)
            for j in range(16):
                lanes = pl.ds(pl.multiple_of((jg * 16 + j) * 128, 128), 128)
                for h in range(2):
                    to = cc * 32 + h * 16
                    ap[to : to + 16, lanes] = r[j * 16 : (j + 1) * 16, h * 128 : (h + 1) * 128]

    loop(0, 4, make_a)

    dl = nt(gs[:, 0:4096], ap[:, 0:4096]) + nt(gs[:, 4096:8192], ap[:, 4096:8192])
    for cq in range(4):
        dlf[cq] = dl[:, cq * 128 : (cq + 1) * 128]
    dsf[...] = jnp.zeros((512, 128), F32)
    for i3 in range(3):
        for cq in range(4):
            dsf[pl.ds(i3 * 4 + cq, 32, stride=16), :] = dlf[cq, pl.ds(i3, 32, stride=3), :]
    sdl[...] = dsf[...].astype(BF16).reshape(32, 16, 128)
    rdl[me_k] = sdl[me_k]

    def send_dl(d):
        k, device = at_k(d)
        send(sdl.at[k], rdl.at[me_k], 3, device)

    loop(1, NK, send_dl)

    arrived(lbuf.at[pl.ds(0, NK - 1)], 1)
    lf[...] = lbuf[...].astype(F32).reshape(512, 128)
    for cq in range(4):
        for i3 in range(3):
            lmf[cq, pl.ds(i3, 32, stride=3), :] = lf[pl.ds(i3 * 4 + cq, 32, stride=16), :]
    for cq in range(4):
        lm[:, cq * 128 : (cq + 1) * 128] = lmf[cq].astype(BF16)
        lt[cq * 128 : (cq + 1) * 128, :] = lmf[cq].T.astype(BF16)

    arrived(bcore, 2)
    bxy[me_p] = bsend[...] + bcore[...]
    loop(1, NXY, lambda d: send(bxy.at[me_p], bxy.at[me_p], 4, at_p(d)[1]))

    def make_b(jg):
        for p in range(8):
            lanes = pl.ds(pl.multiple_of(jg * 2048 + p * 256, 256), 256)
            r = nn(lt[...], gs[:, lanes]).astype(BF16)
            for c in range(32):
                for h in range(2):
                    to = (p * 2 + h) * 16
                    bp[jg, to : to + 16, c * 128 : (c + 1) * 128] = r[c * 16 : (c + 1) * 16, h * 128 : (h + 1) * 128]

    loop(0, 4, make_b)

    dr = jnp.zeros((256, 128), F32)
    for jg in range(4):
        dr = dr + jnp.where(group == jg, nt(bp[jg], w4[...]), 0.0)
    drf[...] = dr * (1.0 / 16.0)
    for s in range(16):
        sdr[s // 2, (s % 2) * 16 : (s % 2) * 16 + 16, :] = drf[pl.ds(s, 16, stride=16), :].astype(BF16)
    rdr[me_q] = sdr[me_q]

    def send_dr(d):
        q, device = at_q(d)
        send(sdr.at[q], rdr.at[me_q], 5, device)

    loop(1, NQ, send_dr)

    for n in range(4):
        lanes = slice(n * 1024, (n + 1) * 1024)
        r = nn(rl[:, 0:256], bp[0, :, lanes])
        for jg in range(1, 4):
            r = r + nn(rl[:, jg * 256 : (jg + 1) * 256], bp[jg, :, lanes])
        gwp[:, lanes] = r
    sgc[...] = gwp[:, pl.ds(pl.multiple_of((1 - core) * 2048, 2048), 2048)].astype(BF16)
    send(sgc, rgc, 6, mate)

    def make_p(jg):
        for p in range(8):
            lanes = pl.ds(pl.multiple_of(jg * 2048 + p * 256, 256), 256)
            r = nn(lm[...], ap[:, lanes])
            for h in range(2):
                pf[pl.ds(jg * 16 + 2 * p + h, 96, stride=64), :] = r[:, h * 128 : (h + 1) * 128]

    loop(0, 2, make_p)

    arrived(rgc, 6)
    for p in range(16):
        lanes = pl.ds(pl.multiple_of(core * 2048 + p * 128, 128), 128)
        half = gwp[:, lanes] + rgc[:, p * 128 : (p + 1) * 128].astype(F32)
        sgx[p] = half.astype(BF16)
    rgx[me_p] = sgx[me_p]

    def send_gx(d):
        p, device = at_p(d)
        send(sgx.at[p], rgx.at[me_p], 7, device)

    loop(1, NXY, send_gx)

    arrived(rdl.at[pl.ds(0, NK - 1)], 3)
    dsum = rdl[0].astype(F32)
    for k in range(1, NK):
        dsum = dsum + rdl[k].astype(F32)
    dsum = dsum.astype(BF16).astype(F32)
    parts = []
    for i3 in range(3):
        row = jnp.concatenate([dsum[i3 * 4 + cq : i3 * 4 + cq + 1, :] for cq in range(4)], axis=1)
        parts.append(jnp.where(lane_s, jnp.broadcast_to(row, (16, 512)), 0.0))
    dleft = nt(jnp.concatenate(parts, axis=0).astype(BF16), fold)
    hat = hat_r[...]
    sm[0] = nn(dleft.T[0:32, :].astype(BF16), hat.astype(BF16))
    back = nt(dleft[:, 0:32].astype(BF16), w1_ref[...])
    out = norm_back(back, hat, inv_r[:, 0:1])
    for h in range(2):
        for i3 in range(3):
            xsf[h, pl.ds(i3, 16, stride=8), :] = out[i3 * 16 : i3 * 16 + 16, h * 128 : (h + 1) * 128]
        for s in range(16):
            grows_ref[s, :, h * 128 : (h + 1) * 128] = xsf[h, s * 8 : s * 8 + 3, :].astype(BF16)

    arrived(bxy.at[pl.ds(0, NXY - 1)], 4)
    total = bxy[0]
    for p in range(1, NXY):
        total = total + bxy[p]
    bz[me_z] = total
    loop(1, NZ, lambda d: send(bz.at[me_z], bz.at[me_z], 8, at_z(d)[1]))

    arrived(rdr.at[pl.ds(0, NQ - 1)], 5)
    dsum = rdr[0].astype(F32)
    for q in range(1, NQ):
        dsum = dsum + rdr[q].astype(F32)
    dsum = dsum.astype(BF16).astype(F32)
    parts = []
    for t in range(2):
        for jg in range(4):
            parts.append(jnp.where(lane_group == jg, dsum[t * 16 : t * 16 + 16, :], 0.0))
    dright = jnp.concatenate(parts, axis=0)
    hat = hat_c[...]
    term = nn(dright.T.astype(BF16), hat.astype(BF16))
    sm[1] = term[0:32, :] + term[32:64, :] + term[64:96, :] + term[96:128, :]
    ssm[...] = sm[1 - core].astype(BF16)
    send(ssm, rsc, 9, mate)
    back = nt(dright.astype(BF16), w2t[...])
    out = norm_back(back, hat, inv_c[:, 0:1])
    gcols_ref[...] = out.reshape(2, 64, 256).astype(BF16)

    arrived(rsc, 9)
    rsx[me_p] = (sm[core] + rsc[...].astype(F32)).astype(BF16)
    loop(1, NXY, lambda d: send(rsx.at[me_p], rsx.at[me_p], 10, at_p(d)[1]))

    arrived(rgx.at[pl.ds(0, NXY - 1)], 7)
    total = rgx[0].astype(F32)
    for p in range(1, NXY):
        total = total + rgx[p].astype(F32)
    rgz[me_z] = total.astype(BF16)
    loop(1, NZ, lambda d: send(rgz.at[me_z], rgz.at[me_z], 11, at_z(d)[1]))

    loop(2, 4, make_p)
    bias = b_ref[...]

    def finish(n):
        for u in range(4):
            rows = pf[pl.ds(pl.multiple_of((4 * n + u) * 64, 64), 64), :]
            po[4 * n + u] = (rows + bias).astype(BF16)

    loop(0, 24, finish)
    store_pair = pltpu.make_async_copy(po, pair_hbm, lsem.at[1])
    store_pair.start()

    arrived(rsx.at[pl.ds(0, NXY - 1)], 10)
    total = rsx[0].astype(F32)
    for p in range(1, NXY):
        total = total + rsx[p].astype(F32)
    rsz[me_z] = total.astype(BF16)
    loop(1, NZ, lambda d: send(rsz.at[me_z], rsz.at[me_z], 12, at_z(d)[1]))

    arrived(rgz.at[pl.ds(0, NZ - 1)], 11)
    total = rgz[0].astype(F32)
    for z in range(1, NZ):
        total = total + rgz[z].astype(F32)
    fgw[core, me_p] = total.astype(BF16)
    loop(1, NXY, lambda d: send(fgw.at[core, me_p], fgw.at[core, me_p], 13, at_p(d)[1]))

    arrived(bz.at[pl.ds(0, NZ - 1)], 8)
    total = bz[0]
    for z in range(1, NZ):
        total = total + bz[z]
    gb_ref[...] = total[0:1, :]

    arrived(rsz.at[pl.ds(0, NZ - 1)], 12)
    total = rsz[0].astype(F32)
    for z in range(1, NZ):
        total = total + rsz[z].astype(F32)
    fsm[core] = total
    send(fsm.at[core], fsm.at[core], 14, mate)
    arrived(fsm.at[0], 14)
    gwl_ref[...] = fsm[0].T
    gwr_ref[...] = fsm[1].T

    arrived(fgw.at[0, pl.ds(0, NXY - 1)], 13)
    send(fgw.at[core], fgw.at[core], 15, mate)
    mine = pl.ds(pl.multiple_of(core * 512, 512), 512)
    gw_ref[mine, :] = fgw[core].astype(F32).reshape(512, 128)
    arrived(fgw.at[0], 15)
    other = pl.ds(pl.multiple_of((1 - core) * 512, 512), 512)
    gw_ref[other, :] = fgw[1 - core].astype(F32).reshape(512, 128)

    store_pair.wait()
    sent(rbuf.at[pl.ds(0, NQ - 1)], 0)
    sent(lbuf.at[pl.ds(0, NK - 1)], 1)
    sent(bsend, 2)
    sent(rdl.at[pl.ds(0, NK - 1)], 3)
    sent(bxy.at[pl.ds(0, NXY - 1)], 4)
    sent(rdr.at[pl.ds(0, NQ - 1)], 5)
    sent(rgc, 6)
    sent(rgx.at[pl.ds(0, NXY - 1)], 7)
    sent(bz.at[pl.ds(0, NZ - 1)], 8)
    sent(ssm, 9)
    sent(rsx.at[pl.ds(0, NXY - 1)], 10)
    sent(rgz.at[pl.ds(0, NZ - 1)], 11)
    sent(rsz.at[pl.ds(0, NZ - 1)], 12)
    sent(fgw.at[0, pl.ds(0, NXY - 1)], 13)
    sent(fsm.at[0], 14)
    sent(fgw.at[0], 15)


SCRATCH = (
    ((96, 64, 128), BF16),
    ((96, 8192), BF16),
    ((6144, 128), F32),
    ((96, 64, 128), BF16),
    ((128, 4096), BF16),
    ((256, 128), BF16),
    ((2, 128, 128), F32),
    ((48, 256), F32),
    ((128, 256), F32),
    ((48, 128), F32),
    ((128, 128), F32),
    ((256, 128), F32),
    ((1024, 128), BF16),
    ((32, 1024), BF16),
    ((512, 8192), BF16),
    ((4, 256, 4096), BF16),
    ((512, 128), F32),
    ((4, 96, 128), F32),
    ((96, 512), BF16),
    ((512, 96), BF16),
    ((4, 96, 128), F32),
    ((512, 128), F32),
    ((256, 128), F32),
    ((32, 4096), F32),
    ((NQ, 32, 128), BF16),
    ((NK, 16, 128), BF16),
    ((NK, 16, 128), BF16),
    ((NK, 16, 128), BF16),
    ((NQ, 32, 128), BF16),
    ((NQ, 32, 128), BF16),
    ((8, 128), F32),
    ((8, 128), F32),
    ((NXY, 8, 128), F32),
    ((NZ, 8, 128), F32),
    ((32, 2048), BF16),
    ((32, 2048), BF16),
    ((NXY, 32, 128), BF16),
    ((NXY, 32, 128), BF16),
    ((NZ, 32, 128), BF16),
    ((2, NXY, 32, 128), BF16),
    ((2, 32, 256), F32),
    ((32, 256), BF16),
    ((32, 256), BF16),
    ((NXY, 32, 256), BF16),
    ((NZ, 32, 256), BF16),
    ((2, 32, 256), F32),
)
SENDS = 16


def local(xs, xc, w1, w2, w, b, g):
    vmem = pl.BlockSpec(memory_space=pltpu.VMEM)
    hbm = pl.BlockSpec(memory_space=pl.ANY)
    pair, grows, gcols, gw, gb, gwl, gwr = pl.pallas_call(
        kernel,
        out_shape=(
            jax.ShapeDtypeStruct((96, 64, 128), BF16),
            jax.ShapeDtypeStruct((16, 3, 256), BF16),
            jax.ShapeDtypeStruct((2, 64, 256), BF16),
            jax.ShapeDtypeStruct((1024, 128), F32),
            jax.ShapeDtypeStruct((1, 128), F32),
            jax.ShapeDtypeStruct((256, 32), F32),
            jax.ShapeDtypeStruct((256, 32), F32),
        ),
        in_specs=[vmem] * 6 + [hbm],
        out_specs=(hbm,) + (vmem,) * 6,
        scratch_shapes=[pltpu.VMEM(shape, dtype) for shape, dtype in SCRATCH]
        + [pltpu.SemaphoreType.DMA((2,))]
        + [pltpu.SemaphoreType.DMA((SENDS,))] * 2,
        compiler_params=pltpu.CompilerParams(
            collective_id=0, has_side_effects=True, vmem_limit_bytes=56 << 20
        ),
        cost_estimate=pl.CostEstimate(flops=3_300_000_000, bytes_accessed=5_000_000, transcendentals=0),
    )(xs, xc, w1, w2, w, b.reshape(1, 128), g)
    return pair, grows, gcols, gw, gb.reshape(128), gwl, gwr


def solution(mesh):
    return jax.shard_map(
        local,
        mesh=mesh,
        in_specs=(
            P(None, ("qrow", "kcol"), None),
            P("qrow", "kcol", None),
            P(),
            P(),
            P(),
            P(),
            P("qrow", "kcol", None),
        ),
        out_specs=(
            P("qrow", "kcol", None),
            P(None, ("qrow", "kcol"), None),
            P("qrow", "kcol", None),
            P(),
            P(),
            P(),
            P(),
        ),
        check_vma=False,
    )
```

time: 826 us -> 66 us (0.08)
  waiting for transfers between devices: 555 us -> 0 us
  local copies, waits for them, and re-layouts: 120 us -> 13.5 us
  blocking collectives: 68 us -> 0 us
  matrix products: 59.7 us -> 0 us
  Pallas kernels: 0 us -> 51.4 us
  between operations: 13.9 us -> 0.65 us
    psum x2 -> x0, waiting for transfers between devices: 483 us -> none  [local(): lax.psum((term_out, term_bias, term_left, term_right), ('qrow', 'kcol'))]
    reduce_scatter x2 -> x0, waiting for transfers between devices: 71.1 us -> none  [the longest x1 71.1 us: local(): lax.psum_scatter((jnp.einsum('ijce,sje->isc', d_outer, right, preferred_e...]
    all_gather x2 -> x0, blocking collectives: 68 us -> none  [the longest x1 39.5 us: local(): left = lax.all_gather(left_local, 'kcol', axis=1, tiled=True)]
    reshape x2 -> x0, local copies, waits for them, and re-layouts: 66.9 us -> none  [the longest x1 34.2 us: local(): d_outer = d_outer.reshape(query_rows, key_cols, chans, chans)]
    dot_general x12 -> x0, matrix products: 59.7 us -> none  [the longest x1 12.4 us: local(): jnp.einsum('ijce,sje->isc', d_outer, right, preferred_element_type=jnp.fl...]
    pallas_call x0 -> x1, Pallas kernels: none -> 51.4 us  [local(): pl.pallas_call(kernel, out_shape=(jax.ShapeDtypeStruct((96, 64, 128), BF1...]
    convert_element_type x4 -> x0, local copies, waits for them, and re-layouts: 46.3 us -> none  [the longest x1 27.8 us: local(): outer.astype(jnp.bfloat16).reshape(query_rows * key_cols, chans * chans)]
  transfers between devices with their start and end apart: 4 -> 0, of which waited for: 3 -> 0; matrix products, arithmetic and copies ran while one was open for 13% -> 0% of each run, Pallas kernels for 0% -> 0%
where the time goes in v1:
time: 66 us; the launch traced here: 65.6 us
  Pallas kernels  51.4 us (78%)
  local copies, waits for them, and re-layouts  13.5 us (20%)
    pallas_call x1, Pallas kernels, local(): pl.pallas_call(kernel, out_shape=(jax.ShapeDtypeStruct((96, 64, 128), BF1...  51.4 us
    unnamed x16, local copies, waits for them, and re-layouts  13.5 us

profile of v1, /device:TPU:1, one launch (start us, length us, event | category | flops | bytes accessed | tf_op | source)
XLA Modules:
  0.0 65.6 jit_solution(17780876362393380593)
XLA Ops:
  0.6 1.4 %copy.14.xs_ref = bf16[16,3,256]{2,1,0:T(4,128)(2,1)} copy(bf16[16,3,256]{2,0,1:T(8,128)(2,1)} %param.7) | data formatting | bytes 49152 | tf_op args[0]
  2.0 1.4 %copy.15.w1_ref = bf16[256,32]{1,0:T(8,128)(2,1)} copy(bf16[256,32]{0,1:T(8,128)(2,1)} %param.9) | data formatting | bytes 32768 | tf_op args[2]
  3.5 1.4 %copy.16.w2_ref = bf16[256,32]{1,0:T(8,128)(2,1)} copy(bf16[256,32]{0,1:T(8,128)(2,1)} %param.10) | data formatting | bytes 32768 | tf_op args[3]
  4.9 51.4 %shard_map.126 = (bf16[96,64,128]{2,1,0:T(8,128)(2,1)}, bf16[16,3,256]{2,1,0:T(4,128)(2,1)}, bf16[2,64,256]{2,1,0:T(8,128)(2,1)}, f32[1024,128]{1,0:T(8,128)}, f...) custom-call(bf16[16,3,256]{2,1,0:T(4,128)(2,1)} %copy.14.xs_ref, bf16[2,64,256]{2,1,0:T(8,128)(2,1)} %xc_ref.1, ...), custom_call_target="tpu_custom_call" | custom-call | flops 3300000000 | bytes 5000000 | tf_op jit(solution)/shard_map/pallas_call | solution.py:470
  56.4 1.4 %copy.17 = bf16[16,3,256]{2,0,1:T(8,128)(2,1)} copy(bf16[16,3,256]{2,1,0:T(4,128)(2,1)} %get-tuple-element.22) | data formatting | bytes 49152
  57.7 1.6 %copy.18 = f32[256,32]{0,1:T(8,128)} copy(f32[256,32]{1,0:T(8,128)} %get-tuple-element.26) | data formatting | bytes 65536
  59.3 1.6 %copy.19 = f32[256,32]{0,1:T(8,128)} copy(f32[256,32]{1,0:T(8,128)} %get-tuple-element.27) | data formatting | bytes 65536
  60.9 0.0 copy-start.1
  60.9 0.0 copy-start
  60.9 0.0 copy-start.2
  60.9 2.7 %copy.24 = bf16[96,64,128]{2,1,0:T(8,128)(2,1)} copy(bf16[96,64,128]{2,1,0:T(8,128)(2,1)} %get-tuple-element.35) | data formatting | bytes 3145728
  63.7 0.0 copy-done.1
  63.7 0.6 copy.25
  64.3 0.0 copy-done
  64.3 0.8 %copy.26 = f32[1024,128]{1,0:T(8,128)} copy(f32[1024,128]{1,0:T(8,128)S(1)} %copy-done) | data formatting | bytes 1048576
  65.1 0.0 copy-done.2
  65.1 0.5 copy.27
Async XLA Ops:
  60.9 2.7 %copy-start.1 = (bf16[2,64,256]{2,1,0:T(8,128)(2,1)S(1)}, bf16[2,64,256]{2,1,0:T(8,128)(2,1)}, u32[]{:S(2)}) copy-start(bf16[2,64,256]{2,1,0:T(8,128)(2,1)} %get-tuple-element.37) | copy-start | bytes 196612
  60.9 3.4 %copy-start = (f32[1024,128]{1,0:T(8,128)S(1)}, f32[1024,128]{1,0:T(8,128)}, u32[]{:S(2)}) copy-start(f32[1024,128]{1,0:T(8,128)} %get-tuple-element.38) | copy-start | bytes 1572868
  60.9 4.2 %copy-start.2 = (f32[1,128]{1,0:T(1,128)S(1)}, f32[1,128]{1,0:T(1,128)}, u32[]{:S(2)}) copy-start(f32[1,128]{1,0:T(1,128)} %get-tuple-element.18) | copy-start | bytes 1540

commit v2 on v1

--- a/solution.py
+++ b/solution.py
@@ -47,9 +47,10 @@
 
 
 def kernel(
-    xs_ref, xc_ref, w1_ref, w2_ref, w_ref, b_ref, g_hbm,
-    pair_hbm, grows_ref, gcols_ref, gw_ref, gb_ref, gwl_ref, gwr_ref,
-    g, gs, pf, po, w4, w2t, xsf, hat_r, hat_c, inv_r, inv_c,
+    xs_hbm, xc_hbm, w1_hbm, w2_hbm, w_hbm, b_hbm, g_hbm,
+    pair_hbm, grows_hbm, gcols_hbm, gw_hbm, gb_hbm, gwl_hbm, gwr_hbm,
+    xs_ref, xc_ref, w1_ref, w2_ref, w_ref, b_ref, grows_ref, gcols_ref, gw_ref, gb_ref,
+    g, gs, pf, po, w4, w2r, hat_r, hat_c, inv_r, inv_c,
     rf, rm, rl, ap, bp, lf, lmf, lm, lt, dlf, dsf, drf, gwp,
     rbuf, lbuf, sdl, rdl, sdr, rdr,
     bsend, bcore, bxy, bz,
@@ -93,8 +94,18 @@
     def sent(ref, n):
         pltpu.make_async_copy(ref, ref, ssem.at[n]).wait()
 
-    load_g = pltpu.make_async_copy(g_hbm, g, lsem.at[0])
-    load_g.start()
+    def fetch(src, dst, n):
+        copy = pltpu.make_async_copy(src, dst, lsem.at[n])
+        copy.start()
+        return copy
+
+    load_xc = fetch(xc_hbm, xc_ref, 0)
+    load_w2 = fetch(w2_hbm, w2_ref, 1)
+    load_xs = fetch(xs_hbm, xs_ref, 2)
+    load_w1 = fetch(w1_hbm, w1_ref, 3)
+    load_g = fetch(g_hbm, g, 4)
+    load_w = fetch(w_hbm, w_ref, 5)
+    load_b = fetch(b_hbm, b_ref, 6)
 
     barrier = pltpu.get_barrier_semaphore()
 
@@ -109,12 +120,14 @@
     lane_s = jnp.bitwise_and(iota((16, 512), 1), 15) == iota((16, 512), 0)
     fold = (lax.shift_right_logical(iota((128, 512), 1), 4) == iota((128, 512), 0)).astype(BF16)
 
-    spread = (jnp.bitwise_and(iota((32, 128), 1), 31) == iota((32, 128), 0)).astype(BF16)
-    w2t[...] = nn(w2_ref[...], spread).astype(BF16)
+    load_xc.wait()
+    load_w2.wait()
+    for jg in range(4):
+        w2r[jg * 32 : (jg + 1) * 32, :] = w2_ref[...]
     hat, inv = normalize(xc_ref[...].astype(F32).reshape(128, 256))
     hat_c[...] = hat
     inv_c[...] = jnp.broadcast_to(inv, (128, 128))
-    right = nn(hat.astype(BF16), w2t[...]).astype(BF16).astype(F32)
+    right = nt(hat.astype(BF16), w2r[...]).astype(BF16).astype(F32)
     tiles = []
     for t in range(2):
         tile = right[t * 64 : t * 64 + 16, :]
@@ -123,20 +136,12 @@
         tiles.append(tile)
     rbuf[me_q] = jnp.concatenate(tiles, axis=0).astype(BF16)
 
-    for h in range(2):
-        for s in range(16):
-            xsf[h, s * 8 : s * 8 + 3, :] = xs_ref[s, :, h * 128 : (h + 1) * 128].astype(F32)
-    rows = jnp.concatenate(
-        [
-            jnp.concatenate([xsf[h, pl.ds(i3, 16, stride=8), :] for h in range(2)], axis=1)
-            for i3 in range(3)
-        ],
-        axis=0,
-    )
-    hat, inv = normalize(rows)
+    load_xs.wait()
+    load_w1.wait()
+    hat, inv = normalize(xs_ref[...].astype(F32).reshape(48, 256))
     hat_r[...] = hat
     inv_r[...] = jnp.broadcast_to(inv, (48, 128))
-    left = nn(hat.astype(BF16), w1_ref[...]).astype(BF16)
+    left = nt(hat.astype(BF16), w1_ref[...]).astype(BF16)
     tile = jnp.zeros((16, 128), F32)
     for i3 in range(3):
         wide = nn(left[i3 * 16 : i3 * 16 + 16, :], fold[0:32, :])
@@ -146,6 +151,7 @@
             tile = jnp.where(iota((16, 128), 0) == i3 * 4 + cq, piece, tile)
     lbuf[me_k] = tile.astype(BF16)
 
+    load_w.wait()
     for c in range(32):
         block = w_ref[c * 32 : (c + 1) * 32, :]
         for jg in range(4):
@@ -299,13 +305,10 @@
     dleft = nt(jnp.concatenate(parts, axis=0).astype(BF16), fold)
     hat = hat_r[...]
     sm[0] = nn(dleft.T[0:32, :].astype(BF16), hat.astype(BF16))
-    back = nt(dleft[:, 0:32].astype(BF16), w1_ref[...])
+    back = nn(dleft[:, 0:32].astype(BF16), w1_ref[...])
     out = norm_back(back, hat, inv_r[:, 0:1])
-    for h in range(2):
-        for i3 in range(3):
-            xsf[h, pl.ds(i3, 16, stride=8), :] = out[i3 * 16 : i3 * 16 + 16, h * 128 : (h + 1) * 128]
-        for s in range(16):
-            grows_ref[s, :, h * 128 : (h + 1) * 128] = xsf[h, s * 8 : s * 8 + 3, :].astype(BF16)
+    grows_ref[...] = out.reshape(3, 16, 256).astype(BF16)
+    store_rows = fetch(grows_ref, grows_hbm, 7)
 
     arrived(bxy.at[pl.ds(0, NXY - 1)], 4)
     total = bxy[0]
@@ -329,9 +332,10 @@
     sm[1] = term[0:32, :] + term[32:64, :] + term[64:96, :] + term[96:128, :]
     ssm[...] = sm[1 - core].astype(BF16)
     send(ssm, rsc, 9, mate)
-    back = nt(dright.astype(BF16), w2t[...])
+    back = nn(dright.astype(BF16), w2r[...])
     out = norm_back(back, hat, inv_c[:, 0:1])
     gcols_ref[...] = out.reshape(2, 64, 256).astype(BF16)
+    store_cols = fetch(gcols_ref, gcols_hbm, 8)
 
     arrived(rsc, 9)
     rsx[me_p] = (sm[core] + rsc[...].astype(F32)).astype(BF16)
@@ -345,6 +349,7 @@
     loop(1, NZ, lambda d: send(rgz.at[me_z], rgz.at[me_z], 11, at_z(d)[1]))
 
     loop(2, 4, make_p)
+    load_b.wait()
     bias = b_ref[...]
 
     def finish(n):
@@ -353,8 +358,7 @@
             po[4 * n + u] = (rows + bias).astype(BF16)
 
     loop(0, 24, finish)
-    store_pair = pltpu.make_async_copy(po, pair_hbm, lsem.at[1])
-    store_pair.start()
+    store_pair = fetch(po, pair_hbm, 9)
 
     arrived(rsx.at[pl.ds(0, NXY - 1)], 10)
     total = rsx[0].astype(F32)
@@ -375,6 +379,7 @@
     for z in range(1, NZ):
         total = total + bz[z]
     gb_ref[...] = total[0:1, :]
+    store_b = fetch(gb_ref, gb_hbm, 10)
 
     arrived(rsz.at[pl.ds(0, NZ - 1)], 12)
     total = rsz[0].astype(F32)
@@ -383,18 +388,21 @@
     fsm[core] = total
     send(fsm.at[core], fsm.at[core], 14, mate)
     arrived(fsm.at[0], 14)
-    gwl_ref[...] = fsm[0].T
-    gwr_ref[...] = fsm[1].T
+    store_wl = fetch(fsm.at[0], gwl_hbm, 11)
+    store_wr = fetch(fsm.at[1], gwr_hbm, 12)
 
     arrived(fgw.at[0, pl.ds(0, NXY - 1)], 13)
     send(fgw.at[core], fgw.at[core], 15, mate)
     mine = pl.ds(pl.multiple_of(core * 512, 512), 512)
     gw_ref[mine, :] = fgw[core].astype(F32).reshape(512, 128)
+    store_mine = fetch(gw_ref.at[mine], gw_hbm.at[mine], 13)
     arrived(fgw.at[0], 15)
     other = pl.ds(pl.multiple_of((1 - core) * 512, 512), 512)
     gw_ref[other, :] = fgw[1 - core].astype(F32).reshape(512, 128)
-
-    store_pair.wait()
+    store_other = fetch(gw_ref.at[other], gw_hbm.at[other], 14)
+
+    for copy in (store_rows, store_cols, store_pair, store_b, store_wl, store_wr, store_mine, store_other):
+        copy.wait()
     sent(rbuf.at[pl.ds(0, NQ - 1)], 0)
     sent(lbuf.at[pl.ds(0, NK - 1)], 1)
     sent(bsend, 2)
@@ -414,13 +422,22 @@
 
 
 SCRATCH = (
+    ((3, 16, 256), BF16),
+    ((2, 64, 256), BF16),
+    ((32, 256), BF16),
+    ((32, 256), BF16),
+    ((1024, 128), BF16),
+    ((1, 128), F32),
+    ((3, 16, 256), BF16),
+    ((2, 64, 256), BF16),
+    ((1024, 128), F32),
+    ((1, 128), F32),
     ((96, 64, 128), BF16),
     ((96, 8192), BF16),
     ((6144, 128), F32),
     ((96, 64, 128), BF16),
     ((128, 4096), BF16),
-    ((256, 128), BF16),
-    ((2, 128, 128), F32),
+    ((128, 256), BF16),
     ((48, 256), F32),
     ((128, 256), F32),
     ((48, 128), F32),
@@ -464,31 +481,60 @@
 SENDS = 16
 
 
+OUTS = (
+    ((96, 64, 128), BF16),
+    ((3, 16, 256), BF16),
+    ((2, 64, 256), BF16),
+    ((1024, 128), F32),
+    ((1, 128), F32),
+    ((32, 256), F32),
+    ((32, 256), F32),
+)
+
+
+def hand_over(*refs):
+    n = len(OUTS)
+    given, taken, held, insem, outsem = refs[:n], refs[n : 2 * n], refs[2 * n : 3 * n], refs[-2], refs[-1]
+    pieces = [(0, pl.ds(k * 24, 24)) for k in range(4)] + [(k, None) for k in range(1, n)]
+    loads, stores = [], []
+    for m, (k, part) in enumerate(pieces):
+        source, slot, target = (r[k] if part is None else r[k].at[part] for r in (given, held, taken))
+        loads.append(pltpu.make_async_copy(source, slot, insem.at[m]))
+        stores.append(pltpu.make_async_copy(slot, target, outsem.at[m]))
+    for load in loads:
+        load.start()
+    for load, store in zip(loads, stores):
+        load.wait()
+        store.start()
+    for store in stores:
+        store.wait()
+
+
 def local(xs, xc, w1, w2, w, b, g):
-    vmem = pl.BlockSpec(memory_space=pltpu.VMEM)
     hbm = pl.BlockSpec(memory_space=pl.ANY)
-    pair, grows, gcols, gw, gb, gwl, gwr = pl.pallas_call(
+    outs = tuple(jax.ShapeDtypeStruct(shape, dtype) for shape, dtype in OUTS)
+    found = pl.pallas_call(
         kernel,
-        out_shape=(
-            jax.ShapeDtypeStruct((96, 64, 128), BF16),
-            jax.ShapeDtypeStruct((16, 3, 256), BF16),
-            jax.ShapeDtypeStruct((2, 64, 256), BF16),
-            jax.ShapeDtypeStruct((1024, 128), F32),
-            jax.ShapeDtypeStruct((1, 128), F32),
-            jax.ShapeDtypeStruct((256, 32), F32),
-            jax.ShapeDtypeStruct((256, 32), F32),
-        ),
-        in_specs=[vmem] * 6 + [hbm],
-        out_specs=(hbm,) + (vmem,) * 6,
+        out_shape=outs,
+        in_specs=[hbm] * 7,
+        out_specs=(hbm,) * 7,
         scratch_shapes=[pltpu.VMEM(shape, dtype) for shape, dtype in SCRATCH]
-        + [pltpu.SemaphoreType.DMA((2,))]
+        + [pltpu.SemaphoreType.DMA((15,))]
         + [pltpu.SemaphoreType.DMA((SENDS,))] * 2,
         compiler_params=pltpu.CompilerParams(
             collective_id=0, has_side_effects=True, vmem_limit_bytes=56 << 20
         ),
         cost_estimate=pl.CostEstimate(flops=3_300_000_000, bytes_accessed=5_000_000, transcendentals=0),
-    )(xs, xc, w1, w2, w, b.reshape(1, 128), g)
-    return pair, grows, gcols, gw, gb.reshape(128), gwl, gwr
+    )(jnp.transpose(xs, (1, 0, 2)), xc, w1.T, w2.T, w, b.reshape(1, 128), g)
+    pair, grows, gcols, gw, gb, gwl, gwr = pl.pallas_call(
+        hand_over,
+        out_shape=outs,
+        in_specs=[hbm] * 7,
+        out_specs=(hbm,) * 7,
+        scratch_shapes=[pltpu.VMEM(shape, dtype) for shape, dtype in OUTS]
+        + [pltpu.SemaphoreType.DMA((len(OUTS) + 3,))] * 2,
+    )(*found)
+    return pair, jnp.transpose(grows, (1, 0, 2)), gcols, gw, gb.reshape(128), gwl.T, gwr.T
 
 
 def solution(mesh):

time: 66 us -> 53.6 us (0.81)
  local copies, waits for them, and re-layouts: 13.5 us -> 0 us
  Pallas kernels: 51.4 us -> 52.8 us
    unnamed x16 -> x0, local copies, waits for them, and re-layouts: 13.5 us -> none
    pallas_call x1 -> x2, Pallas kernels: 51.4 us -> 52.8 us  [the longest x1 50.3 us: local(): pl.pallas_call(kernel, out_shape=outs, in_specs=[hbm] * 7, out_specs=(hbm...]
where the time goes in v2:
time: 53.6 us; the launch traced here: 53.5 us
  Pallas kernels  52.8 us (99%)
  between operations  0.64 us (1%)
    pallas_call x1, Pallas kernels, local(): pl.pallas_call(kernel, out_shape=outs, in_specs=[hbm] * 7, out_specs=(hbm...  50.3 us
    pallas_call x1, Pallas kernels, local(): pl.pallas_call(hand_over, out_shape=outs, in_specs=[hbm] * 7, out_specs=(...  2.53 us

profile of v2, /device:TPU:1, one launch (start us, length us, event | category | flops | bytes accessed | tf_op | source)
XLA Modules:
  0.0 53.5 jit_solution(5592177770166396017)
XLA Ops:
  0.6 50.3 %shard_map.126 = (bf16[96,64,128]{2,1,0:T(8,128)(2,1)}, bf16[3,16,256]{2,1,0:T(8,128)(2,1)}, bf16[2,64,256]{2,1,0:T(8,128)(2,1)}, f32[1024,128]{1,0:T(8,128)}, f...) custom-call(bf16[3,16,256]{2,1,0:T(8,128)(2,1)} %bitcast.10, bf16[2,64,256]{2,1,0:T(8,128)(2,1)} %xc_hbm.1, ...), custom_call_target="tpu_custom_call" | custom-call | flops 3300000000 | bytes 5000000 | tf_op jit(solution)/shard_map/pallas_call | solution.py:516
  50.9 2.5 %shard_map.127 = (bf16[96,64,128]{2,1,0:T(8,128)(2,1)}, bf16[3,16,256]{2,1,0:T(8,128)(2,1)}, bf16[2,64,256]{2,1,0:T(8,128)(2,1)}, f32[1024,128]{1,0:T(8,128)}, f...) custom-call(bf16[96,64,128]{2,1,0:T(8,128)(2,1)} %get-tuple-element.21.refs_0_, ...), custom_call_target="tpu_custom_call" | custom-call | tf_op jit(solution)/shard_map/pallas_call | solution.py:529

commit v3 on v2

--- a/solution.py
+++ b/solution.py
@@ -9,7 +9,7 @@
 MESH = pl.DeviceIdType.MESH
 EPS = 1e-05
 
-NQ, NK, NZ, NXY = 8, 32, 8, 16
+NQ, NZ, NC, NXY, NW = 8, 8, 4, 16, 16
 
 
 def nn(a, b):
@@ -52,10 +52,10 @@
     xs_ref, xc_ref, w1_ref, w2_ref, w_ref, b_ref, grows_ref, gcols_ref, gw_ref, gb_ref,
     g, gs, pf, po, w4, w2r, hat_r, hat_c, inv_r, inv_c,
     rf, rm, rl, ap, bp, lf, lmf, lm, lt, dlf, dsf, drf, gwp,
-    rbuf, lbuf, sdl, rdl, sdr, rdr,
+    rbuf, lbuf, sdl, rdl, szl, rzl, sdr, rdr,
     bsend, bcore, bxy, bz,
     sgc, rgc, sgx, rgx, rgz, fgw,
-    sm, ssm, rsc, rsx, rsz, fsm,
+    ssm, rsx, rsz, fsm, gsm_ref,
     lsem, ssem, rsem,
 ):
     me_q, me_k = lax.axis_index("qrow"), lax.axis_index("kcol")
@@ -63,10 +63,12 @@
     me_x = lax.rem(lax.div(me_k, 2), 2)
     core = lax.rem(me_k, 2)
     me_p = me_x * 8 + me_q
-
-    def at_k(d):
-        k = lax.rem(me_k + d, NK)
-        return k, (me_q, k)
+    me_c = me_x * 2 + core
+    me_w = me_z * 2 + core
+
+    def at_c(d):
+        c = lax.rem(me_c + d, NC)
+        return c, (me_q, me_z * 4 + c)
 
     def at_q(d):
         q = lax.rem(me_q + d, NQ)
@@ -79,6 +81,10 @@
     def at_z(d):
         z = lax.rem(me_z + d, NZ)
         return z, (me_q, z * 4 + me_x * 2 + core)
+
+    def at_zc(d):
+        w = lax.rem(me_w + d, NW)
+        return w, (me_q, lax.div(w, 2) * 4 + me_x * 2 + lax.rem(w, 2))
 
     mate = (me_q, me_k + 1 - 2 * core)
 
@@ -112,9 +118,9 @@
     def greet(device):
         pl.semaphore_signal(barrier, inc=1, device_id=device, device_id_type=MESH)
 
-    loop(1, NK, lambda d: greet(at_k(d)[1]))
-    loop(1, NQ, lambda d: greet(at_q(d)[1]))
-    loop(1, NQ, lambda d: greet((at_q(d)[0], me_z * 4 + (1 - me_x) * 2 + core)))
+    loop(1, NW, lambda d: greet(at_zc(d)[1]))
+    loop(1, NXY, lambda d: greet(at_p(d)[1]))
+    greet((me_q, me_z * 4 + 3 - me_c))
 
     lane_group = lax.shift_right_logical(iota((16, 128), 1), 5)
     lane_s = jnp.bitwise_and(iota((16, 512), 1), 15) == iota((16, 512), 0)
@@ -136,6 +142,9 @@
         tiles.append(tile)
     rbuf[me_q] = jnp.concatenate(tiles, axis=0).astype(BF16)
 
+    pl.semaphore_wait(barrier, NW + NXY - 1)
+    loop(1, NQ, lambda d: send(rbuf.at[me_q], rbuf.at[me_q], 0, at_q(d)[1]))
+
     load_xs.wait()
     load_w1.wait()
     hat, inv = normalize(xs_ref[...].astype(F32).reshape(48, 256))
@@ -149,7 +158,9 @@
         for cq in range(4):
             piece = jnp.broadcast_to(row[:, cq * 128 : (cq + 1) * 128], (16, 128))
             tile = jnp.where(iota((16, 128), 0) == i3 * 4 + cq, piece, tile)
-    lbuf[me_k] = tile.astype(BF16)
+    lbuf[me_c, me_z] = tile.astype(BF16)
+
+    loop(1, NZ, lambda d: send(lbuf.at[me_c, me_z], lbuf.at[me_c, me_z], 1, at_z(d)[1]))
 
     load_w.wait()
     for c in range(32):
@@ -175,11 +186,6 @@
             gs[:, lanes] = pf[pl.ds(4 * n + u, 96, stride=64), :].astype(BF16)
 
     loop(0, 16, turn)
-
-    pl.semaphore_wait(barrier, NK + 2 * NQ - 3)
-
-    loop(1, NQ, lambda d: send(rbuf.at[me_q], rbuf.at[me_q], 0, at_q(d)[1]))
-    loop(1, NK, lambda d: send(lbuf.at[me_k], lbuf.at[me_k], 1, at_k(d)[1]))
     send(bsend, bcore, 2, mate)
 
     arrived(rbuf.at[pl.ds(0, NQ - 1)], 0)
@@ -208,27 +214,34 @@
 
     loop(0, 4, make_a)
 
-    dl = nt(gs[:, 0:4096], ap[:, 0:4096]) + nt(gs[:, 4096:8192], ap[:, 4096:8192])
+    arrived(lbuf.at[0, pl.ds(0, NZ - 1)], 1)
+    loop(1, NC, lambda d: send(lbuf.at[me_c], lbuf.at[me_c], 16, at_c(d)[1]))
+
+    dl = nt(ap[...], gs[...])
     for cq in range(4):
-        dlf[cq] = dl[:, cq * 128 : (cq + 1) * 128]
+        dlf[cq] = dl[cq * 128 : (cq + 1) * 128, :].T
     dsf[...] = jnp.zeros((512, 128), F32)
-    for i3 in range(3):
-        for cq in range(4):
-            dsf[pl.ds(i3 * 4 + cq, 32, stride=16), :] = dlf[cq, pl.ds(i3, 32, stride=3), :]
-    sdl[...] = dsf[...].astype(BF16).reshape(32, 16, 128)
-    rdl[me_k] = sdl[me_k]
+    for c in range(4):
+        for i3 in range(3):
+            for cq in range(4):
+                part = dlf[cq, pl.ds(c * 3 + i3, 8, stride=12), :]
+                dsf[pl.ds(c * 128 + i3 * 4 + cq, 8, stride=16), :] = part
+    sdl[...] = dsf[...].astype(BF16).reshape(4, 8, 16, 128)
+    rdl[me_c] = sdl[me_c]
 
     def send_dl(d):
-        k, device = at_k(d)
-        send(sdl.at[k], rdl.at[me_k], 3, device)
-
-    loop(1, NK, send_dl)
-
-    arrived(lbuf.at[pl.ds(0, NK - 1)], 1)
+        c, device = at_c(d)
+        send(sdl.at[c], rdl.at[me_c], 3, device)
+
+    loop(1, NC, send_dl)
+
+    arrived(lbuf.at[pl.ds(0, NC - 1)], 16)
     lf[...] = lbuf[...].astype(F32).reshape(512, 128)
-    for cq in range(4):
+    for c in range(4):
         for i3 in range(3):
-            lmf[cq, pl.ds(i3, 32, stride=3), :] = lf[pl.ds(i3 * 4 + cq, 32, stride=16), :]
+            for cq in range(4):
+                part = lf[pl.ds(c * 128 + i3 * 4 + cq, 8, stride=16), :]
+                lmf[cq, pl.ds(c * 3 + i3, 8, stride=12), :] = part
     for cq in range(4):
         lm[:, cq * 128 : (cq + 1) * 128] = lmf[cq].astype(BF16)
         lt[cq * 128 : (cq + 1) * 128, :] = lmf[cq].T.astype(BF16)
@@ -248,6 +261,19 @@
 
     loop(0, 4, make_b)
 
+    arrived(rdl.at[pl.ds(0, NC - 1)], 3)
+    total = rdl[0].astype(F32)
+    for c in range(1, NC):
+        total = total + rdl[c].astype(F32)
+    szl[...] = total.astype(BF16)
+    rzl[me_z] = szl[me_z]
+
+    def send_zl(d):
+        z, device = at_z(d)
+        send(szl.at[z], rzl.at[me_z], 17, device)
+
+    loop(1, NZ, send_zl)
+
     dr = jnp.zeros((256, 128), F32)
     for jg in range(4):
         dr = dr + jnp.where(group == jg, nt(bp[jg], w4[...]), 0.0)
@@ -262,23 +288,16 @@
 
     loop(1, NQ, send_dr)
 
-    for n in range(4):
-        lanes = slice(n * 1024, (n + 1) * 1024)
-        r = nn(rl[:, 0:256], bp[0, :, lanes])
-        for jg in range(1, 4):
-            r = r + nn(rl[:, jg * 256 : (jg + 1) * 256], bp[jg, :, lanes])
-        gwp[:, lanes] = r
-    sgc[...] = gwp[:, pl.ds(pl.multiple_of((1 - core) * 2048, 2048), 2048)].astype(BF16)
-    send(sgc, rgc, 6, mate)
-
-    def make_p(jg):
-        for p in range(8):
-            lanes = pl.ds(pl.multiple_of(jg * 2048 + p * 256, 256), 256)
-            r = nn(lm[...], ap[:, lanes])
-            for h in range(2):
-                pf[pl.ds(jg * 16 + 2 * p + h, 96, stride=64), :] = r[:, h * 128 : (h + 1) * 128]
-
-    loop(0, 2, make_p)
+    def make_gw(n):
+        lanes = pl.ds(pl.multiple_of(lax.rem(n + 2 - 2 * core, 4) * 1024, 1024), 1024)
+        gwp[:, lanes] = nn(rl[...], bp[:, :, lanes].reshape(1024, 1024))
+
+        @pl.when(n == 1)
+        def _():
+            sgc[...] = gwp[:, pl.ds(pl.multiple_of((1 - core) * 2048, 2048), 2048)].astype(BF16)
+            send(sgc, rgc, 6, mate)
+
+    loop(0, 4, make_gw)
 
     arrived(rgc, 6)
     for p in range(16):
@@ -293,10 +312,14 @@
 
     loop(1, NXY, send_gx)
 
-    arrived(rdl.at[pl.ds(0, NK - 1)], 3)
-    dsum = rdl[0].astype(F32)
-    for k in range(1, NK):
-        dsum = dsum + rdl[k].astype(F32)
+    def tiled(v, first):
+        for n in range(8):
+            ssm[first + n] = v[n // 2 * 8 : n // 2 * 8 + 8, n % 2 * 128 : n % 2 * 128 + 128]
+
+    arrived(rzl.at[pl.ds(0, NZ - 1)], 17)
+    dsum = rzl[0].astype(F32)
+    for z in range(1, NZ):
+        dsum = dsum + rzl[z].astype(F32)
     dsum = dsum.astype(BF16).astype(F32)
     parts = []
     for i3 in range(3):
@@ -304,7 +327,7 @@
         parts.append(jnp.where(lane_s, jnp.broadcast_to(row, (16, 512)), 0.0))
     dleft = nt(jnp.concatenate(parts, axis=0).astype(BF16), fold)
     hat = hat_r[...]
-    sm[0] = nn(dleft.T[0:32, :].astype(BF16), hat.astype(BF16))
+    tiled(nn(dleft.T[0:32, :].astype(BF16), hat.astype(BF16)), 0)
     back = nn(dleft[:, 0:32].astype(BF16), w1_ref[...])
     out = norm_back(back, hat, inv_r[:, 0:1])
     grows_ref[...] = out.reshape(3, 16, 256).astype(BF16)
@@ -329,17 +352,39 @@
     dright = jnp.concatenate(parts, axis=0)
     hat = hat_c[...]
     term = nn(dright.T.astype(BF16), hat.astype(BF16))
-    sm[1] = term[0:32, :] + term[32:64, :] + term[64:96, :] + term[96:128, :]
-    ssm[...] = sm[1 - core].astype(BF16)
-    send(ssm, rsc, 9, mate)
+    term = term[0:32, :] + term[32:64, :] + term[64:96, :] + term[96:128, :]
+    tiled(term, 8)
+    rsx[me_p] = ssm[me_p]
+
+    def send_small(d):
+        p, device = at_p(d)
+        send(ssm.at[p], rsx.at[me_p], 9, device)
+
+    loop(1, NXY, send_small)
     back = nn(dright.astype(BF16), w2r[...])
     out = norm_back(back, hat, inv_c[:, 0:1])
     gcols_ref[...] = out.reshape(2, 64, 256).astype(BF16)
     store_cols = fetch(gcols_ref, gcols_hbm, 8)
 
-    arrived(rsc, 9)
-    rsx[me_p] = (sm[core] + rsc[...].astype(F32)).astype(BF16)
-    loop(1, NXY, lambda d: send(rsx.at[me_p], rsx.at[me_p], 10, at_p(d)[1]))
+    def make_p(jg):
+        for p in range(8):
+            lanes = pl.ds(pl.multiple_of(jg * 2048 + p * 256, 256), 256)
+            r = nn(lm[...], ap[:, lanes])
+            for h in range(2):
+                pf[pl.ds(jg * 16 + 2 * p + h, 96, stride=64), :] = r[:, h * 128 : (h + 1) * 128]
+
+    loop(0, 4, make_p)
+
+    load_b.wait()
+    bias = b_ref[...]
+
+    def finish(n):
+        for u in range(4):
+            rows = pf[pl.ds(pl.multiple_of((4 * n + u) * 64, 64), 64), :]
+            po[4 * n + u] = (rows + bias).astype(BF16)
+
+    loop(0, 24, finish)
+    store_pair = fetch(po, pair_hbm, 9)
 
     arrived(rgx.at[pl.ds(0, NXY - 1)], 7)
     total = rgx[0].astype(F32)
@@ -348,24 +393,12 @@
     rgz[me_z] = total.astype(BF16)
     loop(1, NZ, lambda d: send(rgz.at[me_z], rgz.at[me_z], 11, at_z(d)[1]))
 
-    loop(2, 4, make_p)
-    load_b.wait()
-    bias = b_ref[...]
-
-    def finish(n):
-        for u in range(4):
-            rows = pf[pl.ds(pl.multiple_of((4 * n + u) * 64, 64), 64), :]
-            po[4 * n + u] = (rows + bias).astype(BF16)
-
-    loop(0, 24, finish)
-    store_pair = fetch(po, pair_hbm, 9)
-
-    arrived(rsx.at[pl.ds(0, NXY - 1)], 10)
-    total = rsx[0].astype(F32)
+    arrived(rsx.at[pl.ds(0, NXY - 1)], 9)
+    total = rsx[0]
     for p in range(1, NXY):
-        total = total + rsx[p].astype(F32)
-    rsz[me_z] = total.astype(BF16)
-    loop(1, NZ, lambda d: send(rsz.at[me_z], rsz.at[me_z], 12, at_z(d)[1]))
+        total = total + rsx[p]
+    rsz[me_w] = total
+    loop(1, NW, lambda d: send(rsz.at[me_w], rsz.at[me_w], 10, at_zc(d)[1]))
 
     arrived(rgz.at[pl.ds(0, NZ - 1)], 11)
     total = rgz[0].astype(F32)
@@ -374,6 +407,13 @@
     fgw[core, me_p] = total.astype(BF16)
     loop(1, NXY, lambda d: send(fgw.at[core, me_p], fgw.at[core, me_p], 13, at_p(d)[1]))
 
+    arrived(rsz.at[pl.ds(0, NW - 1)], 10)
+    total = rsz[0]
+    for w in range(1, NW):
+        total = total + rsz[w]
+    fsm[me_p] = total
+    loop(1, NXY, lambda d: send(fsm.at[me_p], fsm.at[me_p], 14, at_p(d)[1]))
+
     arrived(bz.at[pl.ds(0, NZ - 1)], 8)
     total = bz[0]
     for z in range(1, NZ):
@@ -381,44 +421,40 @@
     gb_ref[...] = total[0:1, :]
     store_b = fetch(gb_ref, gb_hbm, 10)
 
-    arrived(rsz.at[pl.ds(0, NZ - 1)], 12)
-    total = rsz[0].astype(F32)
-    for z in range(1, NZ):
-        total = total + rsz[z].astype(F32)
-    fsm[core] = total
-    send(fsm.at[core], fsm.at[core], 14, mate)
-    arrived(fsm.at[0], 14)
-    store_wl = fetch(fsm.at[0], gwl_hbm, 11)
-    store_wr = fetch(fsm.at[1], gwr_hbm, 12)
-
     arrived(fgw.at[0, pl.ds(0, NXY - 1)], 13)
     send(fgw.at[core], fgw.at[core], 15, mate)
     mine = pl.ds(pl.multiple_of(core * 512, 512), 512)
     gw_ref[mine, :] = fgw[core].astype(F32).reshape(512, 128)
-    store_mine = fetch(gw_ref.at[mine], gw_hbm.at[mine], 13)
+    store_mine = fetch(gw_ref.at[mine], gw_hbm.at[mine], 15)
+    arrived(fsm.at[pl.ds(0, NXY - 1)], 14)
+    for n in range(16):
+        gsm_ref[n // 8, n % 8 // 2 * 8 : n % 8 // 2 * 8 + 8, n % 2 * 128 : n % 2 * 128 + 128] = fsm[n]
+    store_wl = fetch(gsm_ref.at[0], gwl_hbm, 11)
+    store_wr = fetch(gsm_ref.at[1], gwr_hbm, 12)
     arrived(fgw.at[0], 15)
     other = pl.ds(pl.multiple_of((1 - core) * 512, 512), 512)
     gw_ref[other, :] = fgw[1 - core].astype(F32).reshape(512, 128)
-    store_other = fetch(gw_ref.at[other], gw_hbm.at[other], 14)
-
-    for copy in (store_rows, store_cols, store_pair, store_b, store_wl, store_wr, store_mine, store_other):
+    store_other = fetch(gw_ref.at[other], gw_hbm.at[other], 16)
+
+    for copy in (store_rows, store_cols, store_pair, store_b, store_mine, store_other, store_wl, store_wr):
         copy.wait()
     sent(rbuf.at[pl.ds(0, NQ - 1)], 0)
-    sent(lbuf.at[pl.ds(0, NK - 1)], 1)
+    sent(lbuf.at[0, pl.ds(0, NZ - 1)], 1)
     sent(bsend, 2)
-    sent(rdl.at[pl.ds(0, NK - 1)], 3)
+    sent(rdl.at[pl.ds(0, NC - 1)], 3)
     sent(bxy.at[pl.ds(0, NXY - 1)], 4)
     sent(rdr.at[pl.ds(0, NQ - 1)], 5)
     sent(rgc, 6)
     sent(rgx.at[pl.ds(0, NXY - 1)], 7)
     sent(bz.at[pl.ds(0, NZ - 1)], 8)
-    sent(ssm, 9)
-    sent(rsx.at[pl.ds(0, NXY - 1)], 10)
+    sent(rsx.at[pl.ds(0, NXY - 1)], 9)
+    sent(rsz.at[pl.ds(0, NW - 1)], 10)
     sent(rgz.at[pl.ds(0, NZ - 1)], 11)
-    sent(rsz.at[pl.ds(0, NZ - 1)], 12)
     sent(fgw.at[0, pl.ds(0, NXY - 1)], 13)
-    sent(fsm.at[0], 14)
+    sent(fsm.at[pl.ds(0, NXY - 1)], 14)
     sent(fgw.at[0], 15)
+    sent(lbuf.at[pl.ds(0, NC - 1)], 16)
+    sent(rzl.at[pl.ds(0, NZ - 1)], 17)
 
 
 SCRATCH = (
@@ -456,9 +492,11 @@
     ((256, 128), F32),
     ((32, 4096), F32),
     ((NQ, 32, 128), BF16),
-    ((NK, 16, 128), BF16),
-    ((NK, 16, 128), BF16),
-    ((NK, 16, 128), BF16),
+    ((NC, NZ, 16, 128), BF16),
+    ((NC, NZ, 16, 128), BF16),
+    ((NC, NZ, 16, 128), BF16),
+    ((NZ, 16, 128), BF16),
+    ((NZ, 16, 128), BF16),
     ((NQ, 32, 128), BF16),
     ((NQ, 32, 128), BF16),
     ((8, 128), F32),
@@ -471,14 +509,13 @@
     ((NXY, 32, 128), BF16),
     ((NZ, 32, 128), BF16),
     ((2, NXY, 32, 128), BF16),
-    ((2, 32, 256), F32),
-    ((32, 256), BF16),
-    ((32, 256), BF16),
-    ((NXY, 32, 256), BF16),
-    ((NZ, 32, 256), BF16),
+    ((NXY, 8, 128), F32),
+    ((NXY, 8, 128), F32),
+    ((NW, 8, 128), F32),
+    ((NXY, 8, 128), F32),
     ((2, 32, 256), F32),
 )
-SENDS = 16
+SENDS = 18
 
 
 OUTS = (
@@ -519,7 +556,7 @@
         in_specs=[hbm] * 7,
         out_specs=(hbm,) * 7,
         scratch_shapes=[pltpu.VMEM(shape, dtype) for shape, dtype in SCRATCH]
-        + [pltpu.SemaphoreType.DMA((15,))]
+        + [pltpu.SemaphoreType.DMA((17,))]
         + [pltpu.SemaphoreType.DMA((SENDS,))] * 2,
         compiler_params=pltpu.CompilerParams(
             collective_id=0, has_side_effects=True, vmem_limit_bytes=56 << 20

time: 53.6 us -> 52.5 us (0.979)
  Pallas kernels: 52.8 us -> 51.7 us
    pallas_call x1, Pallas kernels: 50.3 us -> 49.2 us  [local(): pl.pallas_call(kernel, out_shape=outs, in_specs=[hbm] * 7, out_specs=(hbm...]
where the time goes in v3:
time: 52.5 us; the launch traced here: 52.3 us
  Pallas kernels  51.7 us (98%)
  between operations  0.64 us (1%)
    pallas_call x1, Pallas kernels, local(): pl.pallas_call(kernel, out_shape=outs, in_specs=[hbm] * 7, out_specs=(hbm...  49.2 us
    pallas_call x1, Pallas kernels, local(): pl.pallas_call(hand_over, out_shape=outs, in_specs=[hbm] * 7, out_specs=(...  2.53 us

profile of v3, /device:TPU:1, one launch (start us, length us, event | category | flops | bytes accessed | tf_op | source)
XLA Modules:
  0.0 52.3 jit_solution(18149437867540194944)
XLA Ops:
  0.6 49.2 %shard_map.126 = (bf16[96,64,128]{2,1,0:T(8,128)(2,1)}, bf16[3,16,256]{2,1,0:T(8,128)(2,1)}, bf16[2,64,256]{2,1,0:T(8,128)(2,1)}, f32[1024,128]{1,0:T(8,128)}, f...) custom-call(bf16[3,16,256]{2,1,0:T(8,128)(2,1)} %bitcast.10, bf16[2,64,256]{2,1,0:T(8,128)(2,1)} %xc_hbm.1, ...), custom_call_target="tpu_custom_call" | custom-call | flops 3300000000 | bytes 5000000 | tf_op jit(solution)/shard_map/pallas_call | solution.py:553
  49.8 2.5 %shard_map.127 = (bf16[96,64,128]{2,1,0:T(8,128)(2,1)}, bf16[3,16,256]{2,1,0:T(8,128)(2,1)}, bf16[2,64,256]{2,1,0:T(8,128)(2,1)}, f32[1024,128]{1,0:T(8,128)}, f...) custom-call(bf16[96,64,128]{2,1,0:T(8,128)(2,1)} %get-tuple-element.21.refs_0_, ...), custom_call_target="tpu_custom_call" | custom-call | tf_op jit(solution)/shard_map/pallas_call | solution.py:566

commit v4 on v3

--- a/solution.py
+++ b/solution.py
@@ -200,19 +200,21 @@
     for jg in range(4):
         rl[:, jg * 256 : (jg + 1) * 256] = rxt[jg * 32 : (jg + 1) * 32, :].astype(BF16)
 
-    def make_a(jg):
-        for cc in range(16):
-            r = nn(
-                rm[pl.ds(pl.multiple_of(jg * 256, 256), 256), :],
-                w4[:, cc * 256 : (cc + 1) * 256],
-            ).astype(BF16)
-            for j in range(16):
-                lanes = pl.ds(pl.multiple_of((jg * 16 + j) * 128, 128), 128)
-                for h in range(2):
-                    to = cc * 32 + h * 16
-                    ap[to : to + 16, lanes] = r[j * 16 : (j + 1) * 16, h * 128 : (h + 1) * 128]
-
-    loop(0, 4, make_a)
+    def make_a(n):
+        for u in range(2):
+            jg = 2 * n + u
+            for cc in range(16):
+                r = nn(
+                    rm[pl.ds(pl.multiple_of(jg * 256, 256), 256), :],
+                    w4[:, cc * 256 : (cc + 1) * 256],
+                ).astype(BF16)
+                for j in range(16):
+                    lanes = pl.ds(pl.multiple_of((jg * 16 + j) * 128, 128), 128)
+                    for h in range(2):
+                        to = cc * 32 + h * 16
+                        ap[to : to + 16, lanes] = r[j * 16 : (j + 1) * 16, h * 128 : (h + 1) * 128]
+
+    loop(0, 2, make_a)
 
     arrived(lbuf.at[0, pl.ds(0, NZ - 1)], 1)
     loop(1, NC, lambda d: send(lbuf.at[me_c], lbuf.at[me_c], 16, at_c(d)[1]))
@@ -250,16 +252,18 @@
     bxy[me_p] = bsend[...] + bcore[...]
     loop(1, NXY, lambda d: send(bxy.at[me_p], bxy.at[me_p], 4, at_p(d)[1]))
 
-    def make_b(jg):
-        for p in range(8):
-            lanes = pl.ds(pl.multiple_of(jg * 2048 + p * 256, 256), 256)
-            r = nn(lt[...], gs[:, lanes]).astype(BF16)
-            for c in range(32):
-                for h in range(2):
-                    to = (p * 2 + h) * 16
-                    bp[jg, to : to + 16, c * 128 : (c + 1) * 128] = r[c * 16 : (c + 1) * 16, h * 128 : (h + 1) * 128]
-
-    loop(0, 4, make_b)
+    def make_b(n):
+        for u in range(2):
+            jg = 2 * n + u
+            for p in range(8):
+                lanes = pl.ds(pl.multiple_of(jg * 2048 + p * 256, 256), 256)
+                r = nn(lt[...], gs[:, lanes]).astype(BF16)
+                for c in range(32):
+                    for h in range(2):
+                        to = (p * 2 + h) * 16
+                        bp[jg, to : to + 16, c * 128 : (c + 1) * 128] = r[c * 16 : (c + 1) * 16, h * 128 : (h + 1) * 128]
+
+    loop(0, 2, make_b)
 
     arrived(rdl.at[pl.ds(0, NC - 1)], 3)
     total = rdl[0].astype(F32)

time: 52.5 us -> 51.8 us (0.987)
  Pallas kernels: 51.7 us -> 51 us
    pallas_call x1, Pallas kernels: 49.2 us -> 48.5 us  [local(): pl.pallas_call(kernel, out_shape=outs, in_specs=[hbm] * 7, out_specs=(hbm...]
where the time goes in v4:
time: 51.8 us; the launch traced here: 51.7 us
  Pallas kernels  51 us (98%)
  between operations  0.64 us (1%)
    pallas_call x1, Pallas kernels, local(): pl.pallas_call(kernel, out_shape=outs, in_specs=[hbm] * 7, out_specs=(hbm...  48.5 us
    pallas_call x1, Pallas kernels, local(): pl.pallas_call(hand_over, out_shape=outs, in_specs=[hbm] * 7, out_specs=(...  2.53 us

profile of v4, /device:TPU:1, one launch (start us, length us, event | category | flops | bytes accessed | tf_op | source)
XLA Modules:
  0.0 51.7 jit_solution(17009327166204109398)
XLA Ops:
  0.6 48.5 %shard_map.126 = (bf16[96,64,128]{2,1,0:T(8,128)(2,1)}, bf16[3,16,256]{2,1,0:T(8,128)(2,1)}, bf16[2,64,256]{2,1,0:T(8,128)(2,1)}, f32[1024,128]{1,0:T(8,128)}, f...) custom-call(bf16[3,16,256]{2,1,0:T(8,128)(2,1)} %bitcast.10, bf16[2,64,256]{2,1,0:T(8,128)(2,1)} %xc_hbm.1, ...), custom_call_target="tpu_custom_call" | custom-call | flops 3300000000 | bytes 5000000 | tf_op jit(solution)/shard_map/pallas_call | solution.py:557
  49.1 2.5 %shard_map.127 = (bf16[96,64,128]{2,1,0:T(8,128)(2,1)}, bf16[3,16,256]{2,1,0:T(8,128)(2,1)}, bf16[2,64,256]{2,1,0:T(8,128)(2,1)}, f32[1024,128]{1,0:T(8,128)}, f...) custom-call(bf16[96,64,128]{2,1,0:T(8,128)(2,1)} %get-tuple-element.21.refs_0_, ...), custom_call_target="tpu_custom_call" | custom-call | tf_op jit(solution)/shard_map/pallas_call | solution.py:570

commit v5 on v4

--- a/solution.py
+++ b/solution.py
@@ -201,6 +201,11 @@
         rl[:, jg * 256 : (jg + 1) * 256] = rxt[jg * 32 : (jg + 1) * 32, :].astype(BF16)
 
     def make_a(n):
+        @pl.when(n == 1)
+        def _():
+            arrived(lbuf.at[0, pl.ds(0, NZ - 1)], 1)
+            loop(1, NC, lambda d: send(lbuf.at[me_c], lbuf.at[me_c], 16, at_c(d)[1]))
+
         for u in range(2):
             jg = 2 * n + u
             for cc in range(16):
@@ -215,9 +220,6 @@
                         ap[to : to + 16, lanes] = r[j * 16 : (j + 1) * 16, h * 128 : (h + 1) * 128]
 
     loop(0, 2, make_a)
-
-    arrived(lbuf.at[0, pl.ds(0, NZ - 1)], 1)
-    loop(1, NC, lambda d: send(lbuf.at[me_c], lbuf.at[me_c], 16, at_c(d)[1]))
 
     dl = nt(ap[...], gs[...])
     for cq in range(4):

time: 51.8 us -> 51.6 us (level)
  no operation moved by 1% of the time
where the time goes in v5:
time: 51.6 us; the launch traced here: 51.5 us
  Pallas kernels  50.9 us (99%)
  between operations  0.64 us (1%)
    pallas_call x1, Pallas kernels, local(): pl.pallas_call(kernel, out_shape=outs, in_specs=[hbm] * 7, out_specs=(hbm...  48.3 us
    pallas_call x1, Pallas kernels, local(): pl.pallas_call(hand_over, out_shape=outs, in_specs=[hbm] * 7, out_specs=(...  2.53 us

profile of v5, /device:TPU:1, one launch (start us, length us, event | category | flops | bytes accessed | tf_op | source)
XLA Modules:
  0.0 51.5 jit_solution(192163108476882815)
XLA Ops:
  0.6 48.3 %shard_map.126 = (bf16[96,64,128]{2,1,0:T(8,128)(2,1)}, bf16[3,16,256]{2,1,0:T(8,128)(2,1)}, bf16[2,64,256]{2,1,0:T(8,128)(2,1)}, f32[1024,128]{1,0:T(8,128)}, f...) custom-call(bf16[3,16,256]{2,1,0:T(8,128)(2,1)} %bitcast.10, bf16[2,64,256]{2,1,0:T(8,128)(2,1)} %xc_hbm.1, ...), custom_call_target="tpu_custom_call" | custom-call | flops 3300000000 | bytes 5000000 | tf_op jit(solution)/shard_map/pallas_call | solution.py:559
  49.0 2.5 %shard_map.127 = (bf16[96,64,128]{2,1,0:T(8,128)(2,1)}, bf16[3,16,256]{2,1,0:T(8,128)(2,1)}, bf16[2,64,256]{2,1,0:T(8,128)(2,1)}, f32[1024,128]{1,0:T(8,128)}, f...) custom-call(bf16[96,64,128]{2,1,0:T(8,128)(2,1)} %get-tuple-element.21.refs_0_, ...), custom_call_target="tpu_custom_call" | custom-call | tf_op jit(solution)/shard_map/pallas_call | solution.py:572
